TPU v7x, 32 devices: a whole 2x2x4 slice. The times are simulated.
32 devices in a mesh: grp: 2 (over y), inst: 4 (over z), tp: 4 (over x, core).
Axes of the slice: x: 2, y: 2, z: 4, core: 2. Of those that a mesh axis runs over, the one named last changes fastest.
Arguments:
- pre_q: bfloat16 [6144, 8192], P(('grp', 'inst'), 'tp'), parts along dimension 0, may hold values from -60 to 60
- pre_kv: bfloat16 [6144, 2, 1024], P(('grp', 'inst'), None, 'tp'), parts along dimension 0, may hold values from -60 to 60
- prompt_len: int32 [8, 4], P(('grp', 'inst')), parts along dimension 0, may hold values from 1 to 384, 768 in all within a row
- page_owner: int32 [192, 1], P('grp'), parts along dimension 0, may hold values from 0 to 3; in each aligned block of 24 rows (0 to 23, 24 to 47, ...) at most 12 rows name the same one
- page_row: int32 [192], P('grp'), parts along dimension 0, may hold values from 0 to 3
- dec_q: bfloat16 [32, 4, 8192], P(('grp', 'inst'), None, 'tp'), parts along dimension 0, may hold values from -60 to 60
- dec_kv: bfloat16 [32, 4, 2, 1024], P(('grp', 'inst'), None, None, 'tp'), parts along dimension 0, may hold values from -60 to 60
- cache_kv: bfloat16 [32, 512, 2, 1024], P(('grp', 'inst'), None, None, 'tp'), parts along dimension 0, may hold values from -60 to 60
- cache_len: int32 [8, 4], P(('grp', 'inst')), parts along dimension 0, may hold values from 1 to 512, 1280 in all within a row
- w_out: bfloat16 [8192, 8192], P('tp', 'inst'), may hold values from -0.0625 to 0.0625
Outputs:
- prefill_out: bfloat16 [6144, 8192], P(('grp', 'inst'), 'tp'), parts along dimension 0
- decode_out: bfloat16 [128, 8192], P(('grp', 'tp'), 'inst'), parts along dimension 0
There are 2 independent parts, one for each index of `grp`. A program takes and returns all parts, laid end to end along the dimension named above; an argument that names none is the same for every part. Nothing has to cross between parts.
Inputs may be any that keep to these rules, and one draw needn't show every extreme that they name: `prompt_len`: on every instance the 4 lengths sum to 768 and the longest is exactly 384. `page_owner`: no instance sends more than 12 of its pages to one owner; in every draw some instance sends exactly 12 pages to one owner. `cache_len`: on every owner the 4 lengths sum to 1280 and the longest is exactly 512.
All inputs are finite; a program needn't handle non-finite values.
Results may differ from a plain program's by a relative error of at most 0.005.
Values may be sent and summed in bfloat16 or wider, within the bound.
A program may use at most 128 MiB of HBM per device.

v0:
```python
import jax
import jax.numpy as jnp
from jax import lax
from jax.sharding import PartitionSpec as P

HEADS = 64
KV_HEADS = 8
HEAD_DIM = 128
BLK = 32


NEG_FILL = -1e30


def split_heads(flat_rows, local_heads):
    return flat_rows.reshape(flat_rows.shape[:-1] + (local_heads, HEADS // KV_HEADS, HEAD_DIM))


def prefill_attention(queries, keyvals, lengths):
    token_count = queries.shape[0]
    local_heads = keyvals.shape[-1] // HEAD_DIM
    prompt_ends = jnp.cumsum(lengths)
    position = jnp.arange(token_count, dtype=jnp.int32)
    prompt_id = jnp.sum((position[:, None] >= prompt_ends[None, :]).astype(jnp.int32), axis=1)
    allowed = (prompt_id[:, None] == prompt_id[None, :]) & (position[:, None] >= position[None, :])
    query_heads = split_heads(queries, local_heads)
    key_rows = keyvals[:, 0].reshape(token_count, local_heads, HEAD_DIM)
    value_rows = keyvals[:, 1].reshape(token_count, local_heads, HEAD_DIM)
    scores = jnp.einsum(
        "qigd,tid->igqt", query_heads, key_rows, preferred_element_type=jnp.float32
    ) * HEAD_DIM ** (-0.5)
    scores = jnp.where(allowed[None, None], scores, NEG_FILL)
    weights = jax.nn.softmax(scores, axis=-1).astype(jnp.bfloat16)
    mixture = jnp.einsum("igqt,tid->qigd", weights, value_rows, preferred_element_type=jnp.float32)
    return mixture.reshape(token_count, queries.shape[1]).astype(jnp.bfloat16)


def slot_partial(queries, page_block):
    local_heads = page_block.shape[-1] // HEAD_DIM
    slot_count, page_len = (page_block.shape[0], page_block.shape[1])
    query_heads = split_heads(queries, local_heads)
    key_rows = page_block[:, :, 0].reshape(slot_count, page_len, local_heads, HEAD_DIM)
    value_rows = (
        page_block[:, :, 1].reshape(slot_count, page_len, local_heads, HEAD_DIM).astype(jnp.float32)
    )
    scores = jnp.einsum(
        "xsigd,xtid->xsigt", query_heads, key_rows, preferred_element_type=jnp.float32
    ) * HEAD_DIM ** (-0.5)
    highest = jnp.max(scores, axis=-1)
    weights = jnp.exp(scores - highest[..., None])
    totals = jnp.sum(weights, axis=-1)
    summed = jnp.einsum("xsigt,xtid->xsigd", weights, value_rows, precision=lax.Precision.HIGHEST)
    return (highest, totals, summed)


def local_partial(queries, cache_rows, lengths, fresh_rows):
    local_heads = cache_rows.shape[-1] // HEAD_DIM
    row_count, step_count = (queries.shape[0], queries.shape[1])
    cache_span = cache_rows.shape[1]
    scale_factor = HEAD_DIM ** (-0.5)
    query_heads = split_heads(queries, local_heads)
    cache_keys = cache_rows[:, :, 0].reshape(row_count, cache_span, local_heads, HEAD_DIM)
    cache_values = (
        cache_rows[:, :, 1]
        .reshape(row_count, cache_span, local_heads, HEAD_DIM)
        .astype(jnp.float32)
    )
    fresh_keys = fresh_rows[:, :, 0].reshape(row_count, step_count, local_heads, HEAD_DIM)
    fresh_values = (
        fresh_rows[:, :, 1]
        .reshape(row_count, step_count, local_heads, HEAD_DIM)
        .astype(jnp.float32)
    )
    cache_scores = (
        jnp.einsum("jsigd,jtid->jsigt", query_heads, cache_keys, preferred_element_type=jnp.float32)
        * scale_factor
    )
    cache_live = jnp.arange(cache_span, dtype=jnp.int32)[None, :] < lengths[:, None]
    cache_scores = jnp.where(cache_live[:, None, None, None, :], cache_scores, NEG_FILL)
    fresh_scores = (
        jnp.einsum("jsigd,jtid->jsigt", query_heads, fresh_keys, preferred_element_type=jnp.float32)
        * scale_factor
    )
    step_index = jnp.arange(step_count, dtype=jnp.int32)
    causal = step_index[None, :] <= step_index[:, None]
    fresh_scores = jnp.where(causal[None, :, None, None, :], fresh_scores, NEG_FILL)
    highest = jnp.maximum(jnp.max(cache_scores, axis=-1), jnp.max(fresh_scores, axis=-1))
    cache_weights = jnp.exp(cache_scores - highest[..., None])
    fresh_weights = jnp.exp(fresh_scores - highest[..., None])
    totals = jnp.sum(cache_weights, axis=-1) + jnp.sum(fresh_weights, axis=-1)
    summed = jnp.einsum(
        "jsigt,jtid->jsigd", cache_weights, cache_values, precision=lax.Precision.HIGHEST
    )
    summed = summed + jnp.einsum(
        "jsigt,jtid->jsigd", fresh_weights, fresh_values, precision=lax.Precision.HIGHEST
    )
    return (highest, totals, summed)


def combine_parts(local_part, remote_part, slot_rows, slot_live):
    highest_l, totals_l, summed_l = local_part
    highest_r, totals_r, summed_r = remote_part
    row_count = highest_l.shape[0]
    belongs = (slot_rows[None, :] == jnp.arange(row_count, dtype=jnp.int32)[:, None]) & slot_live[
        None, :
    ]
    belongs_wide = belongs[:, :, None, None, None]
    remote_best = jnp.max(jnp.where(belongs_wide, highest_r[None], NEG_FILL), axis=1)
    best_score = jnp.maximum(highest_l, remote_best)
    gap_value = jnp.where(belongs_wide, highest_r[None] - best_score[:, None], 0.0)
    factors = jnp.where(belongs_wide, jnp.exp(gap_value), 0.0)
    own_factor = jnp.exp(highest_l - best_score)
    totals = totals_l * own_factor + jnp.sum(factors * totals_r[None], axis=1)
    summed = summed_l * own_factor[..., None] + jnp.einsum(
        "jxsig,xsigd->jsigd", factors, summed_r, precision=lax.Precision.HIGHEST
    )
    return summed / totals[..., None]


def local(
    pre_q, pre_kv, prompt_len, page_owner, page_row, dec_q, dec_kv, cache_kv, cache_len, w_out
):
    prefill_out = prefill_attention(pre_q, pre_kv, prompt_len[0])
    members = lax.axis_size("inst")
    own_index = lax.axis_index("inst")
    owner_table = page_owner.reshape(members, -1)
    row_table = page_row.reshape(members, -1)
    page_count = owner_table.shape[1]
    capacity = max(2, 2 * page_count // members)
    slot_total = members * capacity
    owner_hits = (
        owner_table[:, :, None] == jnp.arange(members, dtype=jnp.int32)[None, None, :]
    ).astype(jnp.int32)
    earlier = jnp.cumsum(owner_hits, axis=1) - owner_hits
    rank_table = jnp.sum(earlier * owner_hits, axis=2)
    my_owners = lax.dynamic_index_in_dim(owner_table, own_index, 0, keepdims=False)
    my_ranks = lax.dynamic_index_in_dim(rank_table, own_index, 0, keepdims=False)
    send_slot = my_owners * capacity + my_ranks
    selector = (send_slot[None, :] == jnp.arange(slot_total, dtype=jnp.int32)[:, None]).astype(
        jnp.bfloat16
    )
    page_tokens = pre_kv.reshape((page_count, BLK) + pre_kv.shape[1:])
    outgoing = jnp.einsum(
        "xp,pbcd->xbcd", selector, page_tokens, preferred_element_type=jnp.float32
    ).astype(jnp.bfloat16)
    matches = (owner_table[:, None, :] == own_index) & (
        rank_table[:, None, :] == jnp.arange(capacity, dtype=jnp.int32)[None, :, None]
    )
    slot_live = jnp.any(matches, axis=2).reshape(slot_total)
    slot_rows = jnp.sum(matches.astype(jnp.int32) * row_table[:, None, :], axis=2).reshape(
        slot_total
    )
    asked_rows = jnp.take(dec_q, slot_rows, axis=0)
    arrived = lax.all_to_all(outgoing, "inst", split_axis=0, concat_axis=0, tiled=True)
    remote_part = slot_partial(asked_rows, arrived)
    local_part = local_partial(dec_q, cache_kv, cache_len[0], dec_kv)
    mixture = combine_parts(local_part, remote_part, slot_rows, slot_live)
    attention = mixture.reshape(dec_q.shape[0] * dec_q.shape[1], dec_q.shape[2]).astype(
        jnp.bfloat16
    )
    projected = jnp.dot(
        lax.all_gather(attention, "inst", axis=0, tiled=True),
        w_out,
        preferred_element_type=jnp.float32,
    )
    decode_out = lax.psum_scatter(projected, "tp", scatter_dimension=0, tiled=True).astype(
        jnp.bfloat16
    )
    return (prefill_out, decode_out)


def solution(mesh):
    return jax.shard_map(
        local,
        mesh=mesh,
        in_specs=(
            P(("grp", "inst"), "tp"),
            P(("grp", "inst"), None, "tp"),
            P(("grp", "inst"), None),
            P("grp", None),
            P("grp"),
            P(("grp", "inst"), None, "tp"),
            P(("grp", "inst"), None, None, "tp"),
            P(("grp", "inst"), None, None, "tp"),
            P(("grp", "inst"), None),
            P("tp", "inst"),
        ),
        out_specs=(P(("grp", "inst"), "tp"), P(("grp", "tp"), "inst")),
        check_vma=False,
    )
```

profile of v0, /device:TPU:0, one launch (start us, length us, event | category | flops | bytes accessed | tf_op | source)
XLA Modules:
  0.0 153.8 jit_solution(15831400441092176028)
XLA Ops:
  7.2 0.5 broadcast.125
  7.7 1.3 reduce.7
  9.2 0.2 select_reduce_fusion.1
  9.5 1.9 %convolution_convert_fusion = bf16[48,32,2,256]{3,0,2,1:T(8,128)(2,1)S(1)} fusion(bf16[24,32,2,256]{3,2,1,0:T(2,128)(2,1)} %bitcast.118, s32[24]{0:T(128)S(1)} %add_bitcast_fusion), kind=kOutput, calls=%fused_computation.17 | convolution fusion | flops 38536320 | bytes 2359392 | tf_op jit(solution)/shard_map/xp,pbcd->xbcd/dot_general | solution.py:143
  11.4 2.8 %copy.142 = bf16[48,32,2,256]{3,2,1,0:T(2,128)(2,1)} copy(bf16[48,32,2,256]{3,0,2,1:T(8,128)(2,1)S(1)} %convolution_convert_fusion) | data formatting | bytes 3145728 | tf_op jit(solution)/shard_map/convert_element_type | solution.py:145
  14.2 6.5 %all-to-all-start = ((bf16[48,32,2,256]{3,2,1,0:T(2,128)(2,1)}), bf16[48,32,2,256]{3,2,1,0:T(2,128)(2,1)S(1)}, u32[]{:S(2)}, u32[]{:S(2)}) async-start(bf16[48,32,2,256]{3,2,1,0:T(2,128)(2,1)} %copy.142), calls=%async_computation | async-start | bytes 3145728 | tf_op jit(solution)/shard_map/all_to_all | solution.py:154
  20.8 2.0 %fusion.66 = (bf16[768,1,256]{2,1,0:T(2,128)(2,1)S(1)}, bf16[768,1,256]{2,1,0:T(2,128)(2,1)}) fusion(bf16[768,2,256]{2,1,0:T(2,128)(2,1)S(1)} %copy-done.1), kind=kLoop, calls=%fused_computation.98 | loop fusion | bytes 1572864 | tf_op jit(solution)/shard_map/slice | solution.py:27
  22.8 0.3 select_reduce_fusion.2
  23.4 0.3 fusion.50
  23.7 0.2 reduce-window.8
  23.9 1.2 fusion.15
  25.5 7.0 %fusion.65 = (bf16[4,512,1,256]{3,2,1,0:T(2,128)(2,1)}, bf16[4,512,1,256]{3,2,1,0:T(2,128)(2,1)}) fusion(bf16[4,512,2,256]{3,2,1,0:T(2,128)(2,1)} %param.17), kind=kLoop, calls=%fused_computation.97 | loop fusion | bytes 4194304 | tf_op jit(solution)/shard_map/slice | solution.py:64
  32.5 5.9 %copy.177 = bf16[4,512,1,256]{1,3,0,2:T(8,128)(2,1)} copy(bf16[4,512,1,256]{3,2,1,0:T(2,128)(2,1)} %get-tuple-element.21) | data formatting | bytes 2097152
  38.4 0.4 fusion.74
  38.9 2.3 %fusion.73 = (f32[4,4,2,8]{3,1,2,0:T(4,128)S(1)}, f32[4,4,2,8,512]{4,3,1,2,0:T(8,128)}) fusion(bf16[4,512,2,128,1]{1,3,4,2,0:T(8,128)(2,1)} %bitcast.123, bf16[4,4,2,8,128]{4,3,2,1,0:T(8,128)(2,1)S(1)} %reshape.244, pred[4,512]{1,0:T(4,128)(4,1)S(1)} %iota_compare_fusion.5), kind=kOutput, calls=%fused_computation.101 | convolution fusion | flops 33947392 | bytes 1641472 | tf_op jit(solution)/shard_map/jsigd,jtid->jsigt/dot_general | solution.py:75
  41.2 1.6 %copy.129 = bf16[768,1,256]{0,2,1:T(8,128)(2,1)} copy(bf16[768,1,256]{2,1,0:T(2,128)(2,1)S(1)} %copy-done.2) | data formatting | bytes 786432 | tf_op jit(solution)/shard_map/slice | solution.py:28
  42.8 1.7 %copy.176 = bf16[768,1,256]{0,2,1:T(8,128)(2,1)} copy(bf16[768,1,256]{2,1,0:T(2,128)(2,1)S(1)} %get-tuple-element.22) | data formatting | bytes 786432
  44.5 4.6 %copy.179 = bf16[96,8,16,128]{3,2,1,0:T(8,128)(2,1)} copy(bf16[96,8,16,128]{3,1,2,0:T(8,128)(2,1)} %bitcast.119) | data formatting | bytes 6291456
  49.0 1.2 gather_fusion
  50.3 1.4 gather.7
  51.7 5.8 %copy.178 = bf16[4,512,1,256]{1,3,0,2:T(8,128)(2,1)} copy(bf16[4,512,1,256]{3,2,1,0:T(2,128)(2,1)} %get-tuple-element.20) | data formatting | bytes 2097152
  57.5 19.8 %fusion.68 = (f32[2,8,768]{2,1,0:T(8,128)}, f32[2,8,768,768]{2,3,1,0:T(8,128)}) fusion(bf16[768,2,128,1]{0,2,3,1:T(8,128)(2,1)S(1)} %bitcast.131, pred[768,768]{0,1:T(8,128)(4,1)S(1)} %copy-done.5, bf16[768,2,8,128]{3,2,1,0:T(8,128)(2,1)} %bitcast.120), kind=kOutput, calls=%fused_computation.100 | convolution fusion | flops 2453668608 | bytes 41926656 | tf_op jit(solution)/shard_map/sub | solution.py:33
  77.3 6.7 %slice_reduce_fusion = (bf16[48,32,256]{2,1,0:T(8,128)(2,1)S(1)}, bf16[48,32,256]{2,1,0:T(8,128)(2,1)S(1)}) fusion(bf16[48,32,2,256]{3,2,1,0:T(2,128)(2,1)S(1)} %all-to-all-done), kind=kLoop, calls=%fused_computation.18 | loop fusion | bytes 3145728 | tf_op jit(solution)/shard_map/slice | solution.py:44
  84.0 1.1 reshape_squeeze.30
  85.0 2.1 %bitcast_reduce_fusion = (f32[48,4,2,8]{3,1,2,0:T(4,128)S(1)}, f32[48,2,32,4,8]{2,4,3,1,0:T(8,128)S(1)}) fusion(bf16[48,4,2,8,128]{4,3,2,1,0:T(8,128)(2,1)} %gather.7, pred[48]{0:T(512)(128)(4,1)S(1)} %compare_and_fusion, bf16[48,32,2,128,1]{3,2,1,0,4:T(2,128)(2,1)} %bitcast.124), kind=kOutput, calls=%fused_computation.21 | convolution fusion | flops 25752576 | bytes 1978416 | tf_op jit(solution)/shard_map/xsigd,xtid->xsigt/dot_general | solution.py:46
  87.2 0.1 copy.146
  87.3 0.2 select_reduce_fusion
  87.4 0.1 copy.147
  87.6 0.7 fusion.64
  88.3 0.7 fusion.45
  88.9 0.9 fusion.46
  89.9 0.2 reshape_squeeze.31
  90.1 1.1 fusion.20
  91.2 2.6 %convolution_bitcast_fusion = f32[48,4,2,8,128]{4,3,1,2,0:T(8,128)S(1)} fusion(f32[48,2,32,4,8]{2,4,3,1,0:T(8,128)} %copy-done.3, bf16[48,32,2,128,1]{3,2,1,0,4:T(2,128)(2,1)S(1)} %bitcast.125, f32[48,4,2,8]{3,1,2,0:T(4,128)S(1)} %get-tuple-element.28), kind=kOutput, calls=%fused_computation.26 | convolution fusion | flops 151093248 | bytes 2764800 | tf_op jit(solution)/shard_map/xsigt,xtid->xsigd/dot_general | solution.py:52
  93.8 1.0 copy.149
  94.7 0.7 copy.152
  95.5 3.2 %fusion.18 = f32[4,2,8,128,4]{3,4,2,1,0:T(4,128)S(1)} fusion(f32[48,4,2,8,128]{4,3,1,2,0:T(8,128)S(1)} %convolution_bitcast_fusion, f32[4,4,2,8]{0,3,2,1:T(8,128)S(1)} %copy.149, f32[48,4,2,8]{0,3,2,1:T(8,128)} %copy-done.7, pred[4,48]{1,0:T(4,128)(4,1)} %copy-done.13), kind=kOutput, calls=%fused_computation.23 | convolution fusion | flops 18911232 | bytes 1717440 | tf_op jit(solution)/shard_map/jxsig,xsigd->jsigd/dot_general | solution.py:114
  98.7 1.0 multiply_reduce_fusion
  99.7 0.1 copy.153
  99.9 0.3 fusion.36
  100.1 0.7 multiply_add_fusion
  100.9 1.2 fusion.28
  102.1 14.3 %all_gather.3 = bf16[64,2048]{1,0:T(8,128)(2,1)S(1)} all-gather(bf16[16,2048]{1,0:T(8,128)(2,1)S(1)} %convert_element_type.43), channel_id=1, replica_groups=mesh['grp'=2,'inst'=4,'tp'=4] {'inst'}, dimensions={0}, use_global_device_ids=true | all-gather | bytes 327680 | tf_op jit(solution)/shard_map/all_gather | solution.py:162
  116.5 5.8 %fusion.75 = f32[64,2048]{1,0:T(8,128)} fusion(bf16[64,2048]{1,0:T(8,128)(2,1)S(1)} %all_gather.3, bf16[2048,2048]{1,0:T(8,128)(2,1)} %param.19), kind=kOutput, calls=%fused_computation.103 | convolution fusion | flops 536870912 | bytes 9175040 | tf_op jit(solution)/shard_map/dot_general | solution.py:161
  122.3 13.5 %fusion.16 = bf16[2,8,768,128]{2,3,1,0:T(8,128)(2,1)S(1)} fusion(bf16[768,2,128,1]{0,2,3,1:T(8,128)(2,1)S(1)} %bitcast.130, f32[2,8,768,768]{2,3,1,0:T(8,128)} %get-tuple-element.27, f32[2,8,768]{2,1,0:T(8,128)} %get-tuple-element.26), kind=kOutput, calls=%fused_computation.16 | convolution fusion | flops 2436366336 | bytes 41336832 | tf_op jit(solution)/shard_map/igqt,tid->qigd/dot_general | solution.py:34
  135.8 2.9 %copy.155 = bf16[768,2048]{1,0:T(8,128)(2,1)} copy(bf16[768,2048]{0,1:T(8,128)(2,1)S(1)} %bitcast.121) | data formatting | bytes 6291456
  138.7 6.7 %reduce-scatter.2.cloned.1.call-done = f32[16,2048]{1,0:T(8,128)} async-done(((f32[64,2048]{1,0:T(8,128)}), f32[16,2048]{1,0:T(8,128)}) %reduce-scatter.2.cloned.1.call-update) | async-done | bytes 131088 | tf_op jit(solution)/shard_map/reduce_scatter | solution.py:166
  145.4 1.5 %convert_element_type.44 = bf16[16,2048]{1,0:T(8,128)(2,1)} convert(f32[16,2048]{1,0:T(8,128)} %reduce-scatter.2.cloned.1.call-done) | non-fusion elementwise | flops 32768 | bytes 196608 | tf_op jit(solution)/shard_map/convert_element_type | solution.py:166
  (59 shorter events, 1.2 us)
Async XLA Ops:
  14.2 6.5 %copy-start.1 = (bf16[768,2,256]{2,1,0:T(2,128)(2,1)S(1)}, bf16[768,2,256]{2,1,0:T(2,128)(2,1)}, u32[]{:S(2)}) copy-start(bf16[768,2,256]{2,1,0:T(2,128)(2,1)} %param.11) | copy-start | bytes 2359300
  14.2 63.0 %all-to-all-start = ((bf16[48,32,2,256]{3,2,1,0:T(2,128)(2,1)}), bf16[48,32,2,256]{3,2,1,0:T(2,128)(2,1)S(1)}, u32[]{:S(2)}, u32[]{:S(2)}) async-start(bf16[48,32,2,256]{3,2,1,0:T(2,128)(2,1)} %copy.142), calls=%async_computation | async-start | bytes 3145728 | tf_op jit(solution)/shard_map/all_to_all | solution.py:154
  20.7 2.1 %copy-start.14 = (s32[96]{0:T(128)S(1)}, s32[96]{0:T(128)}, u32[]{:S(2)}) copy-start(s32[96]{0:T(128)} %param.14) | copy-start | bytes 1156
  20.7 3.0 %copy-start.16 = (s32[1,4]{1,0:T(1,128)S(1)}, s32[1,4]{1,0:T(1,128)}, u32[]{:S(2)}) copy-start(s32[1,4]{1,0:T(1,128)} %param.12) | copy-start | bytes 52
  20.7 4.5 %copy-start = (bf16[4,4,2048]{2,1,0:T(4,128)(2,1)S(1)}, bf16[4,4,2048]{2,1,0:T(4,128)(2,1)}, u32[]{:S(2)}) copy-start(bf16[4,4,2048]{2,1,0:T(4,128)(2,1)} %param.15) | copy-start | bytes 196612
  20.7 4.5 %copy-start.12 = (bf16[4,4,2,256]{3,2,1,0:T(2,128)(2,1)S(1)}, bf16[4,4,2,256]{3,2,1,0:T(2,128)(2,1)}, u32[]{:S(2)}) copy-start(bf16[4,4,2,256]{3,2,1,0:T(2,128)(2,1)} %param.16) | copy-start | bytes 49156
  20.7 124.7 %reduce-scatter.2.cloned.1.call-start = ((), (), s32[]{:S(2)}) async-start(), calls=%async_computation.2 | async-start | bytes 655360 | tf_op jit(solution)/shard_map/reduce_scatter | solution.py:166
  25.5 61.8 %copy-start.13 = (pred[4,48]{1,0:T(4,128)(4,1)}, pred[4,48]{1,0:T(4,128)(4,1)S(1)}, u32[]{:S(2)}) copy-start(pred[4,48]{1,0:T(4,128)(4,1)S(1)} %fusion.58) | copy-start | bytes 580
  32.5 5.9 %copy-start.15 = (s32[1,4]{1,0:T(1,128)S(1)}, s32[1,4]{1,0:T(1,128)}, u32[]{:S(2)}) copy-start(s32[1,4]{1,0:T(1,128)} %param.18) | copy-start | bytes 52
  32.5 8.7 %copy-start.2 = (bf16[768,1,256]{2,1,0:T(2,128)(2,1)S(1)}, bf16[768,1,256]{2,1,0:T(2,128)(2,1)}, u32[]{:S(2)}) copy-start(bf16[768,1,256]{2,1,0:T(2,128)(2,1)} %get-tuple-element.23) | copy-start | bytes 1179652
  50.3 7.2 %copy-start.5 = (pred[768,768]{0,1:T(8,128)(4,1)S(1)}, pred[768,768]{0,1:T(8,128)(4,1)}, u32[]{:S(2)}) copy-start(pred[768,768]{0,1:T(8,128)(4,1)} %fusion.15) | copy-start | bytes 1769476
  50.3 7.2 %copy-start.9 = (bf16[768,1,256]{0,2,1:T(8,128)(2,1)S(1)}, bf16[768,1,256]{0,2,1:T(8,128)(2,1)}, u32[]{:S(2)}) copy-start(bf16[768,1,256]{0,2,1:T(8,128)(2,1)} %copy.176) | copy-start | bytes 1179652
  87.1 4.0 %copy-start.3 = (f32[48,2,32,4,8]{2,4,3,1,0:T(8,128)}, f32[48,2,32,4,8]{2,4,3,1,0:T(8,128)S(1)}, u32[]{:S(2)}) copy-start(f32[48,2,32,4,8]{2,4,3,1,0:T(8,128)S(1)} %get-tuple-element.29) | copy-start | bytes 1179652
  87.3 2.6 %copy-start.7 = (f32[48,4,2,8]{0,3,2,1:T(8,128)}, f32[48,4,2,8]{0,3,2,1:T(8,128)S(1)}, u32[]{:S(2)}) copy-start(f32[48,4,2,8]{0,3,2,1:T(8,128)S(1)} %copy.146) | copy-start | bytes 36868
  93.7 6.1 %copy-start.6 = (f32[4,4,2,8,512]{4,3,1,2,0:T(8,128)S(1)}, f32[4,4,2,8,512]{4,3,1,2,0:T(8,128)}, u32[]{:S(2)}) copy-start(f32[4,4,2,8,512]{4,3,1,2,0:T(8,128)} %get-tuple-element.31) | copy-start | bytes 1572868
  93.8 6.4 %copy-start.10 = (f32[4,8,1,8]{3,1,2,0:T(8,128)S(1)}, f32[4,8,1,8]{3,1,2,0:T(8,128)}, u32[]{:S(2)}) copy-start(f32[4,8,1,8]{3,1,2,0:T(8,128)} %get-tuple-element.34) | copy-start | bytes 3076
  93.8 7.1 %copy-start.4 = (bf16[4,512,1,256]{1,3,0,2:T(8,128)(2,1)S(1)}, bf16[4,512,1,256]{1,3,0,2:T(8,128)(2,1)}, u32[]{:S(2)}) copy-start(bf16[4,512,1,256]{1,3,0,2:T(8,128)(2,1)} %copy.178) | copy-start | bytes 3145732
  93.8 7.1 %copy-start.11 = (f32[4,2,4,8,128]{4,3,2,1,0:T(8,128)S(1)}, f32[4,2,4,8,128]{4,3,2,1,0:T(8,128)}, u32[]{:S(2)}) copy-start(f32[4,2,4,8,128]{4,3,2,1,0:T(8,128)} %fusion.46) | copy-start | bytes 393220
  116.5 5.8 %copy-start.8 = (bf16[768,1,256]{0,2,1:T(8,128)(2,1)S(1)}, bf16[768,1,256]{0,2,1:T(8,128)(2,1)}, u32[]{:S(2)}) copy-start(bf16[768,1,256]{0,2,1:T(8,128)(2,1)} %copy.129) | copy-start | bytes 1179652
Sparse Core Ops, SparseCore 0:
  122.4 22.9 reduce-scatter.1
where the time goes:
time: 155 us; the launch traced here: 154 us
  matrix products  53.7 us (35%)
  local copies, waits for them, and re-layouts  48.1 us (31%)
  between operations  14.4 us (9%)
  blocking collectives  14.3 us (9%)
  other arithmetic  10 us (6%)
  waiting for transfers between devices  6.77 us (4%)
  starting transfers between devices  6.49 us (4%)
    unnamed x40, local copies, waits for them, and re-layouts  21.4 us
    sub x1, matrix products, prefill_attention(): weights = jax.nn.softmax(scores, axis=-1).astype(jnp.bfloat16)  19.8 us
    all_gather x1, blocking collectives, local(): lax.all_gather(attention, 'inst', axis=0, tiled=True)  14.3 us
    dot_general x1, matrix products, prefill_attention(): jnp.einsum('igqt,tid->qigd', weights, value_rows, preferred_element_type=...  13.5 us
    slice x1, local copies, waits for them, and re-layouts, local_partial(): cache_rows[:, :, 1].reshape(row_count, cache_span, local_heads, HEAD_DIM)  7 us
    reduce_scatter x1, waiting for transfers between devices, local(): lax.psum_scatter(projected, 'tp', scatter_dimension=0, tiled=True)  6.75 us
    slice x1, local copies, waits for them, and re-layouts, slot_partial(): page_block[:, :, 1].reshape(slot_count, page_len, local_heads, HEAD_DIM)  6.69 us
    all_to_all x1, starting transfers between devices, local(): lax.all_to_all(outgoing, 'inst', split_axis=0, concat_axis=0, tiled=True)  6.45 us
  transfers between devices with their start and end apart: 2, of which 1 were waited for; matrix products, arithmetic and copies ran while one was open for 47% of the time, Pallas kernels for 0%

commit v1 on v0

v1 whole, which is shorter than its diff:
```python
import functools
import math

import jax
import jax.numpy as jnp
from jax import lax
from jax.experimental import pallas as pl
from jax.experimental.pallas import tpu as pltpu
from jax.sharding import PartitionSpec as P

HEADS = 64
KV_HEADS = 8
GROUP = HEADS // KV_HEADS
HD = 128
BLK = 32
PMAX = 384
QB = 128
NEG = -1e30
C2 = HD ** -0.5 * math.log2(math.e)
MESH = pl.DeviceIdType.MESH


def dot_nt(a, b):
    return lax.dot_general(a, b, (((1,), (1,)), ((), ())), preferred_element_type=jnp.float32)


def dot_tn(a, b):
    return lax.dot_general(a, b, (((0,), (0,)), ((), ())), preferred_element_type=jnp.float32)


def loop(lo, hi, body, carry):
    if hi - lo <= 4:
        for k in range(lo, hi):
            carry = body(k, carry)
        return carry
    return lax.fori_loop(lo, hi, body, carry)


def each(lo, hi, body):
    def step(k, carry):
        body(k)
        return carry

    loop(lo, hi, step, 0)


def kernel(
    n, m,
    pre_q, pre_kv, prompt_len, page_owner, page_row, dq, dec_kv, cache, cache_len, w_out,
    pre_out, dec_out,
    pq, pkv, ckv, w, ob,
    pk, pv, ck, cv, gid, bias, sl,
    qall, rpo, rml, spo, sml, aall, pf, pj, rp,
    lsem, osem, qs, qr, os_, or_, ms, mr, as_, ar, js, jr,
):
    me = lax.axis_index("inst")
    mt = lax.axis_index("tp")
    ptok = pre_q.shape[0]
    nh = pre_kv.shape[2] // HD
    rdev, cap = cache.shape[0], cache.shape[1]
    rows = dq.shape[0]
    steps = rows // rdev
    qv = GROUP * rows
    pages = ptok // BLK

    loads = [
        pltpu.make_async_copy(src, dst, lsem.at[i])
        for i, (src, dst) in enumerate(((cache, ckv), (pre_kv, pkv), (pre_q, pq), (w_out, w)))
    ]
    for c in loads:
        c.start()

    barrier = pltpu.get_barrier_semaphore()
    each(1, n, lambda k: pl.semaphore_signal(
        barrier, inc=1, device_id={"inst": lax.rem(me + k, n)}, device_id_type=MESH))
    each(1, m, lambda k: pl.semaphore_signal(
        barrier, inc=1, device_id={"tp": lax.rem(mt + k, m)}, device_id_type=MESH))
    pl.semaphore_wait(barrier, n + m - 2)

    def q_copy(k):
        return pltpu.make_async_remote_copy(
            src_ref=dq, dst_ref=qall.at[k], send_sem=qs.at[k], recv_sem=qr.at[k],
            device_id={"inst": lax.rem(me + k, n)}, device_id_type=MESH)

    def o_copy(k):
        return pltpu.make_async_remote_copy(
            src_ref=spo.at[k], dst_ref=rpo.at[k], send_sem=os_.at[k], recv_sem=or_.at[k],
            device_id={"inst": lax.rem(me - k + n, n)}, device_id_type=MESH)

    def m_copy(k):
        return pltpu.make_async_remote_copy(
            src_ref=sml.at[k], dst_ref=rml.at[k], send_sem=ms.at[k], recv_sem=mr.at[k],
            device_id={"inst": lax.rem(me - k + n, n)}, device_id_type=MESH)

    def a_copy(k, owner):
        block = aall.at[pl.ds(pl.multiple_of(owner * rows, rows), rows)]
        return pltpu.make_async_remote_copy(
            src_ref=block, dst_ref=block, send_sem=as_.at[k], recv_sem=ar.at[k],
            device_id={"inst": lax.rem(me + k, n)}, device_id_type=MESH)

    rpt = n * rows // m

    def j_copy(k):
        dest = lax.rem(mt + k, m)
        return pltpu.make_async_remote_copy(
            src_ref=pj.at[pl.ds(pl.multiple_of(dest * rpt, rpt), rpt)], dst_ref=rp.at[k],
            send_sem=js.at[k], recv_sem=jr.at[k], device_id={"tp": dest}, device_id_type=MESH)

    each(1, n, lambda k: q_copy(k).start())

    lane = lax.broadcasted_iota(jnp.int32, (1, qv), 1)
    lane_row = lax.rem(lane, rows) // steps
    lane_step = lax.rem(lane, steps)

    def stacked(ref, h):
        return jnp.concatenate(
            [ref[:, (h * GROUP + g) * HD:(h * GROUP + g + 1) * HD] for g in range(GROUP)], axis=0)

    loads[0].wait()
    chunk = 256
    for h in range(nh):
        cols = slice(h * HD, (h + 1) * HD)

        def split(j, carry, h=h, cols=cols):
            r, t = j // (cap // chunk), lax.rem(j, cap // chunk) * chunk
            at = pl.multiple_of(j * chunk, chunk)
            ck[h, pl.ds(at, chunk), :] = ckv[r, pl.ds(t, chunk), 0, cols]
            cv[h, pl.ds(at, chunk), :] = ckv[r, pl.ds(t, chunk), 1, cols]
            return carry

        lax.fori_loop(0, rdev * cap // chunk, split, 0)
        ck[h, rdev * cap:, :] = dec_kv[:, 0, cols]
        cv[h, rdev * cap:, :] = dec_kv[:, 1, cols]

    local = []
    slot = lax.broadcasted_iota(jnp.int32, (cap, qv), 0)
    fresh = lax.broadcasted_iota(jnp.int32, (rows, qv), 0)
    for h in range(nh):
        query = stacked(dq, h)
        best = jnp.full((1, qv), NEG, jnp.float32)
        for r in range(rdev):
            s = dot_nt(ck[h, r * cap:(r + 1) * cap, :], query)
            s = jnp.where((slot < cache_len[0, r]) & (lane_row == r), s, NEG)
            sl[r * cap:(r + 1) * cap, :] = s
            best = jnp.maximum(best, jnp.max(s, axis=0, keepdims=True))
        s = dot_nt(ck[h, rdev * cap:, :], query)
        s = jnp.where((fresh // steps == lane_row) & (lax.rem(fresh, steps) <= lane_step), s, NEG)
        sl[rdev * cap:, :] = s
        best = jnp.maximum(best, jnp.max(s, axis=0, keepdims=True))
        total = jnp.zeros((1, qv), jnp.float32)
        mixed = jnp.zeros((HD, qv), jnp.float32)
        for r in range(rdev + 1):
            at = slice(r * cap, min((r + 1) * cap, rdev * cap + rows))
            p = jnp.exp2((sl[at, :] - best) * C2)
            total = total + jnp.sum(p, axis=0, keepdims=True)
            mixed = mixed + dot_tn(cv[h, at, :], p.astype(jnp.bfloat16))
        local.append((best, total, mixed))

    loads[1].wait()
    for h in range(nh):
        cols = slice(h * HD, (h + 1) * HD)

        def part(j, carry, h=h, cols=cols):
            t = pl.multiple_of(j * chunk, chunk)
            pk[h, pl.ds(t, chunk), :] = pkv[pl.ds(t, chunk), 0, cols]
            pv[h, pl.ds(t, chunk), :HD] = pkv[pl.ds(t, chunk), 1, cols]
            pv[h, pl.ds(t, chunk), HD:] = jnp.ones((chunk, HD), jnp.bfloat16)
            return carry

        lax.fori_loop(0, ptok // chunk, part, 0)
    for p in range(pages):
        at = me * pages + p
        gid[p * BLK:(p + 1) * BLK, :] = jnp.full(
            (BLK, qv), page_owner[at] * rdev + page_row[at], jnp.int32)

    def page_part(k, q_ref, o_ref, m_ref):
        owner = lax.rem(me - k + n, n)
        mine = gid[...] == owner * rdev + lane_row
        for h in range(nh):
            s = dot_nt(pk[h], stacked(q_ref, h))
            s = jnp.where(mine, s, NEG)
            best = jnp.max(s, axis=0, keepdims=True)
            p = jnp.where(mine, jnp.exp2((s - best) * C2), 0.0)
            m_ref[2 * h:2 * h + 1, :] = best
            m_ref[2 * h + 1:2 * h + 2, :] = jnp.sum(p, axis=0, keepdims=True)
            o_ref[h] = dot_tn(pv[h, :, :HD], p.astype(jnp.bfloat16)).astype(jnp.bfloat16)

    def remote_part(k, carry):
        q_copy(k).wait_recv()
        page_part(k, qall.at[k], spo.at[k], sml.at[k])
        o_copy(k).start()
        m_copy(k).start()
        return carry

    lax.fori_loop(1, n, remote_part, 0)
    page_part(0, dq, rpo.at[0], rml.at[0])

    def prefill(h, blocks):
        for i in blocks:
            lo, hi = max(0, i - PMAX // QB) * QB, (i + 1) * QB
            wide = hi - lo
            token = lax.broadcasted_iota(jnp.int32, (QB, HD), 0) + i * QB
            first = jnp.zeros((QB, HD), jnp.int32)
            end = 0
            for j in range(prompt_len.shape[1]):
                length = prompt_len[0, j]
                end = end + length
                first = jnp.where(token >= end, first + length, first)
            for b in range(wide // HD):
                key = lax.broadcasted_iota(jnp.int32, (QB, HD), 1) + (lo + b * HD)
                bias[:, b * HD:(b + 1) * HD] = jnp.where(
                    (key >= first) & (key <= token), 0.0, NEG)

            def head(g, carry):
                at = pl.multiple_of((h * GROUP + g) * HD, HD)
                s = dot_nt(pq[i * QB:(i + 1) * QB, pl.ds(at, HD)], pk[h, lo:hi, :])
                s = s + bias[:, :wide]
                best = jnp.max(s, axis=1, keepdims=True)
                p = jnp.exp2((s - best) * C2).astype(jnp.bfloat16)
                o = jnp.dot(p, pv[h, lo:hi, :], preferred_element_type=jnp.float32)
                ob[i * QB:(i + 1) * QB, pl.ds(at, HD)] = (o[:, :HD] / o[:, HD:]).astype(jnp.bfloat16)
                return carry

            lax.fori_loop(0, GROUP, head, 0, unroll=2)

    blocks = ptok // QB
    work = [(h, i) for h in range(nh) for i in range(blocks)]
    cut1, cut2 = len(work) * 5 // 12, len(work) * 10 // 12

    def out_copy(i):
        return pltpu.make_async_copy(
            ob.at[i * QB:(i + 1) * QB], pre_out.at[i * QB:(i + 1) * QB], osem.at[i])

    def do(items):
        for h, i in items:
            prefill(h, [i])
            if h == nh - 1:
                out_copy(i).start()

    loads[2].wait()
    do(work[:cut1])

    each(1, n, lambda k: (o_copy(k).wait_recv(), m_copy(k).wait_recv()))
    for h in range(nh):
        best0, total0, mixed0 = local[h]
        best = loop(0, n, lambda k, b: jnp.maximum(b, rml[k, 2 * h:2 * h + 1, :]), best0)
        f0 = jnp.exp2((best0 - best) * C2)

        def add(k, carry):
            total, mixed = carry
            f = jnp.exp2((rml[k, 2 * h:2 * h + 1, :] - best) * C2)
            return (total + f * rml[k, 2 * h + 1:2 * h + 2, :],
                    mixed + f * rpo[k, h].astype(jnp.float32))

        total, mixed = loop(0, n, add, (total0 * f0, mixed0 * f0))
        att = jnp.transpose(mixed / total).astype(jnp.bfloat16)
        for g in range(GROUP):
            c = (h * GROUP + g) * HD
            aall[pl.ds(pl.multiple_of(me * rows, rows), rows), c:c + HD] = att[g * rows:(g + 1) * rows]
    each(1, n, lambda k: a_copy(k, me).start())

    do(work[cut1:cut2])

    loads[3].wait()
    each(1, n, lambda k: a_copy(k, lax.rem(me - k + n, n)).wait_recv())
    wide = w.shape[1]
    piece = min(512, wide)

    def project(j, carry):
        c = pl.ds(pl.multiple_of(j * piece, piece), piece)
        acc = jnp.dot(aall[...], w[:, c], preferred_element_type=jnp.float32)
        pf[:, c] = acc
        pj[:, c] = acc.astype(jnp.bfloat16)
        return carry

    lax.fori_loop(0, wide // piece, project, 0)
    each(1, m, lambda k: j_copy(k).start())

    do(work[cut2:])

    each(1, m, lambda k: j_copy(k).wait_recv())
    acc = loop(1, m, lambda k, a: a + rp[k].astype(jnp.float32),
               pf[pl.ds(pl.multiple_of(mt * rpt, rpt), rpt), :])
    dec_out[...] = acc.astype(jnp.bfloat16)

    each(1, n, lambda k: (q_copy(k).wait_send(), o_copy(k).wait_send(),
                          m_copy(k).wait_send(), a_copy(k, me).wait_send()))
    each(1, m, lambda k: j_copy(k).wait_send())
    for i in range(blocks):
        out_copy(i).wait()


def local(pre_q, pre_kv, prompt_len, page_owner, page_row, dec_q, dec_kv, cache_kv, cache_len, w_out):
    n, m = lax.axis_size("inst"), lax.axis_size("tp")
    ptok, width = pre_q.shape
    nh = pre_kv.shape[2] // HD
    rdev, steps = dec_q.shape[0], dec_q.shape[1]
    rows = rdev * steps
    qv = GROUP * rows
    slots = rdev * cache_kv.shape[1] + rows
    bf, f32 = jnp.bfloat16, jnp.float32
    any_, vmem, smem = (pl.BlockSpec(memory_space=s) for s in (pl.ANY, pltpu.VMEM, pltpu.SMEM))
    outw = w_out.shape[1]
    rpt = n * rows // m
    dma = pltpu.SemaphoreType.DMA
    return pl.pallas_call(
        functools.partial(kernel, n, m),
        out_shape=(jax.ShapeDtypeStruct((ptok, width), bf), jax.ShapeDtypeStruct((rpt, outw), bf)),
        in_specs=[any_, any_, smem, smem, smem, vmem, vmem, any_, smem, any_],
        out_specs=(any_, vmem),
        scratch_shapes=[
            pltpu.VMEM(pre_q.shape, bf), pltpu.VMEM(pre_kv.shape, bf), pltpu.VMEM(cache_kv.shape, bf),
            pltpu.VMEM(w_out.shape, bf), pltpu.VMEM((ptok, width), bf),
            pltpu.VMEM((nh, ptok, HD), bf), pltpu.VMEM((nh, ptok, 2 * HD), bf),
            pltpu.VMEM((nh, slots, HD), bf), pltpu.VMEM((nh, slots, HD), bf),
            pltpu.VMEM((ptok, qv), jnp.int32), pltpu.VMEM((QB, PMAX + QB), f32), pltpu.VMEM((slots, qv), f32),
            pltpu.VMEM((n, rows, width), bf),
            pltpu.VMEM((n, nh, HD, qv), bf), pltpu.VMEM((n, 8, qv), f32),
            pltpu.VMEM((n, nh, HD, qv), bf), pltpu.VMEM((n, 8, qv), f32),
            pltpu.VMEM((n * rows, width), bf), pltpu.VMEM((n * rows, outw), f32),
            pltpu.VMEM((n * rows, outw), bf), pltpu.VMEM((m, rpt, outw), bf),
            dma((4,)), dma((ptok // QB,)),
            dma((n,)), dma((n,)), dma((n,)), dma((n,)), dma((n,)), dma((n,)), dma((n,)), dma((n,)),
            dma((m,)), dma((m,)),
        ],
        compiler_params=pltpu.CompilerParams(
            collective_id=0, has_side_effects=True, vmem_limit_bytes=56 << 20),
    )(pre_q, pre_kv, prompt_len, page_owner.reshape(-1), page_row,
      dec_q.reshape(rows, width), dec_kv.reshape((rows,) + dec_kv.shape[2:]), cache_kv, cache_len, w_out)


def solution(mesh):
    return jax.shard_map(
        local,
        mesh=mesh,
        in_specs=(
            P(("grp", "inst"), "tp"),
            P(("grp", "inst"), None, "tp"),
            P(("grp", "inst"), None),
            P("grp", None),
            P("grp"),
            P(("grp", "inst"), None, "tp"),
            P(("grp", "inst"), None, None, "tp"),
            P(("grp", "inst"), None, None, "tp"),
            P(("grp", "inst"), None),
            P("tp", "inst"),
        ),
        out_specs=(P(("grp", "inst"), "tp"), P(("grp", "tp"), "inst")),
        check_vma=False,
    )
```

time: 155 us -> 56.3 us (0.36)
  matrix products: 53.7 us -> 0 us
  Pallas kernels: 0 us -> 49.3 us
  local copies, waits for them, and re-layouts: 48.1 us -> 6.12 us
  blocking collectives: 14.3 us -> 0 us
  between operations: 14.4 us -> 0.65 us
  other arithmetic: 10 us -> 0 us
  waiting for transfers between devices: 6.77 us -> 0 us
  starting transfers between devices: 6.49 us -> 0 us
    pallas_call x0 -> x1, Pallas kernels: none -> 49.3 us  [local(): pl.pallas_call(functools.partial(kernel, n, m), out_shape=(jax.ShapeDtype...]
    dot_general x10 -> x0, matrix products: 33.9 us -> none  [the longest x1 13.5 us: prefill_attention(): jnp.einsum('igqt,tid->qigd', weights, value_rows, preferred_element_type=...]
    sub x1 -> x0, matrix products: 19.8 us -> none  [prefill_attention(): weights = jax.nn.softmax(scores, axis=-1).astype(jnp.bfloat16)]
    slice x5 -> x0, local copies, waits for them, and re-layouts: 17.3 us -> none  [the longest x1 7 us: local_partial(): cache_rows[:, :, 1].reshape(row_count, cache_span, local_heads, HEAD_DIM)]
    unnamed x40 -> x4, local copies, waits for them, and re-layouts: 21.4 us -> 4.63 us
    all_gather x1 -> x0, blocking collectives: 14.3 us -> none  [local(): lax.all_gather(attention, 'inst', axis=0, tiled=True)]
    reduce_scatter x1 -> x0, waiting for transfers between devices: 6.75 us -> none  [local(): lax.psum_scatter(projected, 'tp', scatter_dimension=0, tiled=True)]
    all_to_all x1 -> x0, starting transfers between devices: 6.45 us -> none  [local(): lax.all_to_all(outgoing, 'inst', split_axis=0, concat_axis=0, tiled=True)]
  transfers between devices with their start and end apart: 2 -> 0, of which waited for: 1 -> 0; matrix products, arithmetic and copies ran while one was open for 47% -> 0% of each run, Pallas kernels for 0% -> 0%
where the time goes in v1:
time: 56.3 us; the launch traced here: 56.1 us
  Pallas kernels  49.3 us (88%)
  local copies, waits for them, and re-layouts  6.12 us (11%)
  between operations  0.65 us (1%)
    pallas_call x1, Pallas kernels, local(): pl.pallas_call(functools.partial(kernel, n, m), out_shape=(jax.ShapeDtype...  49.3 us
    unnamed x4, local copies, waits for them, and re-layouts  4.63 us
    reshape x1, local copies, waits for them, and re-layouts, local(): dec_q.reshape(rows, width)  1.49 us

profile of v1, /device:TPU:0, one launch (start us, length us, event | category | flops | bytes accessed | tf_op | source)
XLA Modules:
  0.0 56.1 jit_solution(10766021872803398227)
XLA Ops:
  0.6 1.5 %reshape.14.dq = bf16[16,2048]{1,0:T(8,128)(2,1)} reshape(bf16[4,4,2048]{2,1,0:T(4,128)(2,1)} %param.15) | data formatting | bytes 131072 | tf_op jit(solution)/shard_map/reshape | solution.py:329
  2.1 49.3 %shard_map.113 = (bf16[768,2048]{1,0:T(8,128)(2,1)}, bf16[16,2048]{1,0:T(8,128)(2,1)}) custom-call(bf16[768,2048]{1,0:T(8,128)(2,1)} %pre_q.1, bf16[768,2,256]{2,1,0:T(2,128)(2,1)} %pre_kv.1, s32[1,4]{1,0:T(1,128)} %prompt_len.1, s32[96]{0:T(128)} %bitcast.3, s32[96]{0:T(128)} %page_row.1, bf16[16,2048]{1,0:T(8,128)(2,1)} %reshape.14.dq, ...), custom_call_target="tpu_custom_call" | custom-call | tf_op jit(solution)/shard_map/pallas_call | solution.py:306
  51.4 0.0 copy-start
  51.4 4.0 %copy.14 = bf16[768,2048]{1,0:T(8,128)(2,1)} copy(bf16[768,2048]{1,0:T(8,128)(2,1)} %get-tuple-element.4) | data formatting | bytes 6291456
  55.4 0.0 copy-done
  55.4 0.6 %copy.15 = bf16[16,2048]{1,0:T(8,128)(2,1)} copy(bf16[16,2048]{1,0:T(8,128)(2,1)S(1)} %copy-done) | data formatting | bytes 131072
Async XLA Ops:
  51.4 4.0 %copy-start = (bf16[16,2048]{1,0:T(8,128)(2,1)S(1)}, bf16[16,2048]{1,0:T(8,128)(2,1)}, u32[]{:S(2)}) copy-start(bf16[16,2048]{1,0:T(8,128)(2,1)} %get-tuple-element.5) | copy-start | bytes 196612

commit v2 on v1

--- a/solution.py
+++ b/solution.py
@@ -58,8 +58,8 @@
     ptok = pre_q.shape[0]
     nh = pre_kv.shape[2] // HD
     rdev, cap = cache.shape[0], cache.shape[1]
-    rows = dq.shape[0]
-    steps = rows // rdev
+    steps = dq.shape[1]
+    rows = rdev * steps
     qv = GROUP * rows
     pages = ptok // BLK
 
@@ -75,7 +75,6 @@
         barrier, inc=1, device_id={"inst": lax.rem(me + k, n)}, device_id_type=MESH))
     each(1, m, lambda k: pl.semaphore_signal(
         barrier, inc=1, device_id={"tp": lax.rem(mt + k, m)}, device_id_type=MESH))
-    pl.semaphore_wait(barrier, n + m - 2)
 
     def q_copy(k):
         return pltpu.make_async_remote_copy(
@@ -105,8 +104,6 @@
         return pltpu.make_async_remote_copy(
             src_ref=pj.at[pl.ds(pl.multiple_of(dest * rpt, rpt), rpt)], dst_ref=rp.at[k],
             send_sem=js.at[k], recv_sem=jr.at[k], device_id={"tp": dest}, device_id_type=MESH)
-
-    each(1, n, lambda k: q_copy(k).start())
 
     lane = lax.broadcasted_iota(jnp.int32, (1, qv), 1)
     lane_row = lax.rem(lane, rows) // steps
@@ -114,7 +111,8 @@
 
     def stacked(ref, h):
         return jnp.concatenate(
-            [ref[:, (h * GROUP + g) * HD:(h * GROUP + g + 1) * HD] for g in range(GROUP)], axis=0)
+            [ref[:, :, (h * GROUP + g) * HD:(h * GROUP + g + 1) * HD].reshape(rows, HD)
+             for g in range(GROUP)], axis=0)
 
     loads[0].wait()
     chunk = 256
@@ -185,16 +183,6 @@
             m_ref[2 * h + 1:2 * h + 2, :] = jnp.sum(p, axis=0, keepdims=True)
             o_ref[h] = dot_tn(pv[h, :, :HD], p.astype(jnp.bfloat16)).astype(jnp.bfloat16)
 
-    def remote_part(k, carry):
-        q_copy(k).wait_recv()
-        page_part(k, qall.at[k], spo.at[k], sml.at[k])
-        o_copy(k).start()
-        m_copy(k).start()
-        return carry
-
-    lax.fori_loop(1, n, remote_part, 0)
-    page_part(0, dq, rpo.at[0], rml.at[0])
-
     def prefill(h, blocks):
         for i in blocks:
             lo, hi = max(0, i - PMAX // QB) * QB, (i + 1) * QB
@@ -221,24 +209,38 @@
                 ob[i * QB:(i + 1) * QB, pl.ds(at, HD)] = (o[:, :HD] / o[:, HD:]).astype(jnp.bfloat16)
                 return carry
 
-            lax.fori_loop(0, GROUP, head, 0, unroll=2)
+            lax.fori_loop(0, GROUP, head, 0, unroll=GROUP)
 
     blocks = ptok // QB
-    work = [(h, i) for h in range(nh) for i in range(blocks)]
-    cut1, cut2 = len(work) * 5 // 12, len(work) * 10 // 12
+    stages = [[], [blocks - 1, 0], [blocks - 2, blocks - 3], list(range(blocks - 4, 0, -1))]
 
     def out_copy(i):
         return pltpu.make_async_copy(
             ob.at[i * QB:(i + 1) * QB], pre_out.at[i * QB:(i + 1) * QB], osem.at[i])
 
-    def do(items):
-        for h, i in items:
-            prefill(h, [i])
-            if h == nh - 1:
-                out_copy(i).start()
+    def do(stage):
+        for i in stages[stage]:
+            for h in range(nh):
+                prefill(h, [i])
+            out_copy(i).start()
 
     loads[2].wait()
-    do(work[:cut1])
+    do(0)
+    pl.semaphore_wait(barrier, n + m - 2)
+    each(1, n, lambda k: q_copy(k).start())
+    do(1)
+
+    def remote_part(k, carry):
+        q_copy(k).wait_recv()
+        page_part(k, qall.at[k], spo.at[k], sml.at[k])
+        o_copy(k).start()
+        m_copy(k).start()
+        return carry
+
+    lax.fori_loop(1, n, remote_part, 0)
+    page_part(0, dq, rpo.at[0], rml.at[0])
+
+    do(2)
 
     each(1, n, lambda k: (o_copy(k).wait_recv(), m_copy(k).wait_recv()))
     for h in range(nh):
@@ -259,7 +261,7 @@
             aall[pl.ds(pl.multiple_of(me * rows, rows), rows), c:c + HD] = att[g * rows:(g + 1) * rows]
     each(1, n, lambda k: a_copy(k, me).start())
 
-    do(work[cut1:cut2])
+    do(3)
 
     loads[3].wait()
     each(1, n, lambda k: a_copy(k, lax.rem(me - k + n, n)).wait_recv())
@@ -275,8 +277,6 @@
 
     lax.fori_loop(0, wide // piece, project, 0)
     each(1, m, lambda k: j_copy(k).start())
-
-    do(work[cut2:])
 
     each(1, m, lambda k: j_copy(k).wait_recv())
     acc = loop(1, m, lambda k, a: a + rp[k].astype(jnp.float32),
@@ -314,7 +314,7 @@
             pltpu.VMEM((nh, ptok, HD), bf), pltpu.VMEM((nh, ptok, 2 * HD), bf),
             pltpu.VMEM((nh, slots, HD), bf), pltpu.VMEM((nh, slots, HD), bf),
             pltpu.VMEM((ptok, qv), jnp.int32), pltpu.VMEM((QB, PMAX + QB), f32), pltpu.VMEM((slots, qv), f32),
-            pltpu.VMEM((n, rows, width), bf),
+            pltpu.VMEM((n,) + dec_q.shape, bf),
             pltpu.VMEM((n, nh, HD, qv), bf), pltpu.VMEM((n, 8, qv), f32),
             pltpu.VMEM((n, nh, HD, qv), bf), pltpu.VMEM((n, 8, qv), f32),
             pltpu.VMEM((n * rows, width), bf), pltpu.VMEM((n * rows, outw), f32),
@@ -326,7 +326,7 @@
         compiler_params=pltpu.CompilerParams(
             collective_id=0, has_side_effects=True, vmem_limit_bytes=56 << 20),
     )(pre_q, pre_kv, prompt_len, page_owner.reshape(-1), page_row,
-      dec_q.reshape(rows, width), dec_kv.reshape((rows,) + dec_kv.shape[2:]), cache_kv, cache_len, w_out)
+      dec_q, dec_kv.reshape((rows,) + dec_kv.shape[2:]), cache_kv, cache_len, w_out)
 
 
 def solution(mesh):

time: 56.3 us -> 46.3 us (0.82)
  Pallas kernels: 49.3 us -> 40.8 us
  local copies, waits for them, and re-layouts: 6.12 us -> 4.63 us
    pallas_call x1, Pallas kernels: 49.3 us -> 40.8 us  [local(): pl.pallas_call(functools.partial(kernel, n, m), out_shape=(jax.ShapeDtype...]
    reshape x1 -> x0, local copies, waits for them, and re-layouts: 1.49 us -> none  [local(): dec_q.reshape(rows, width)]
where the time goes in v2:
time: 46.3 us; the launch traced here: 46.1 us
  Pallas kernels  40.8 us (88%)
  local copies, waits for them, and re-layouts  4.63 us (10%)
  between operations  0.65 us (1%)
    pallas_call x1, Pallas kernels, local(): pl.pallas_call(functools.partial(kernel, n, m), out_shape=(jax.ShapeDtype...  40.8 us
    unnamed x4, local copies, waits for them, and re-layouts  4.63 us

profile of v2, /device:TPU:0, one launch (start us, length us, event | category | flops | bytes accessed | tf_op | source)
XLA Modules:
  0.0 46.1 jit_solution(1033712348695168308)
XLA Ops:
  0.6 40.8 %shard_map.113 = (bf16[768,2048]{1,0:T(8,128)(2,1)}, bf16[16,2048]{1,0:T(8,128)(2,1)}) custom-call(bf16[768,2048]{1,0:T(8,128)(2,1)} %pre_q.1, bf16[768,2,256]{2,1,0:T(2,128)(2,1)} %pre_kv.1, s32[1,4]{1,0:T(1,128)} %prompt_len.1, s32[96]{0:T(128)} %bitcast.3, s32[96]{0:T(128)} %page_row.1, bf16[4,4,2048]{2,1,0:T(4,128)(2,1)} %dq.1, ...), custom_call_target="tpu_custom_call" | custom-call | tf_op jit(solution)/shard_map/pallas_call | solution.py:306
  41.4 0.0 copy-start
  41.4 4.0 %copy.14 = bf16[768,2048]{1,0:T(8,128)(2,1)} copy(bf16[768,2048]{1,0:T(8,128)(2,1)} %get-tuple-element.4) | data formatting | bytes 6291456
  45.4 0.0 copy-done
  45.4 0.6 %copy.15 = bf16[16,2048]{1,0:T(8,128)(2,1)} copy(bf16[16,2048]{1,0:T(8,128)(2,1)S(1)} %copy-done) | data formatting | bytes 131072
Async XLA Ops:
  41.4 4.0 %copy-start = (bf16[16,2048]{1,0:T(8,128)(2,1)S(1)}, bf16[16,2048]{1,0:T(8,128)(2,1)}, u32[]{:S(2)}) copy-start(bf16[16,2048]{1,0:T(8,128)(2,1)} %get-tuple-element.5) | copy-start | bytes 196612
